TPU v7x, 128 devices: a whole 4x4x4 slice. The times are simulated.
128 devices in a mesh: section: 8 (over y, x_lo), dp: 16 (over z, x_hi, core).
Axes of the slice: x: 4 (x_hi: 2, x_lo: 2; x = x_hi * 2 + x_lo), y: 4, z: 4, core: 2. Of those that a mesh axis runs over, the one named last changes fastest.
Arguments:
- fwd_input: bfloat16 [8, 2048, 8192], P('section', 'dp'), may hold values from -6 to 6
- bwd_input: bfloat16 [8, 2048, 8192], P('section', 'dp'), may hold values from -6 to 6
- cotangent: bfloat16 [8, 2048, 8192], P('section', 'dp'), may hold values from -6 to 6
- send_buffer: bfloat16 [8, 48, 64, 8192], P('section', 'dp'), may hold values from -6 to 6
- recv_buffer: bfloat16 [8, 48, 64, 8192], P('section', 'dp'), may hold values from -6 to 6
- fwd_ids: int32 [8, 32], P('section', 'dp'), may hold values from 0 to 2
- recv_ids: int32 [8, 32], P('section', 'dp'), may hold values from 0 to 2
- norm_gain: float32 [8, 8192], P('section'), may hold values from 0.1 to 1.9
- w_gate: bfloat16 [8, 8192, 128], P('section'), may hold values from -0.0625 to 0.0625
- w_in: bfloat16 [8, 8192, 128], P('section'), may hold values from -0.0625 to 0.0625
- w_out: bfloat16 [8, 8192, 128], P('section'), may hold values from -0.5 to 0.5
Outputs:
- next_input: bfloat16 [8, 2048, 8192], P('section', 'dp')
- send_rows: bfloat16 [8, 2048, 8192], P('section', 'dp')
- next_cotangent: bfloat16 [8, 2048, 8192], P('section', 'dp')
- weight_grads: float32 [8, 8192, 384], P('section', 'dp')
- gain_grad: float32 [8, 8192], P('section', 'dp')
Inputs may be any that keep to these rules, and one draw needn't show every extreme that they name: `fwd_ids`: slot numbers within the replica's own 3 stored samples; repeats may occur. `recv_ids`: slot numbers within the replica's own 3 stored samples; repeats may occur.
All inputs are finite; a program needn't handle non-finite values. Where the computation divides by a largest or mean magnitude, that divisor is 1e-20 or more.
Results may differ from a plain program's by a relative error of at most 0.019.
Values may be sent and summed in bfloat16 or wider, within the bound.
A program may use at most 192 MiB of HBM per device.

v0:
```python
import jax
import jax.numpy as jnp
from jax import lax
from jax.sharding import PartitionSpec as P

BLOCK = 128


EPS_NORM = 1e-05
EPS_SCALE = 1e-06


def passed_along(block, axis, distance):
    devices = range(lax.axis_size(axis))
    route = [(i - distance, i) for i in devices if i - distance in devices]
    return lax.ppermute(block, axis, route)


def contract_rows(left, right):
    return lax.dot_general(
        left, right, (((0,), (0,)), ((), ())), preferred_element_type=jnp.float32
    )


def contract_cols(left, right):
    return lax.dot_general(
        left, right, (((1,), (1,)), ((), ())), preferred_element_type=jnp.float32
    )


def adapter_inner(inputs, gain_row, w_gate, w_in):
    wide = inputs.astype(jnp.float32)
    recip = lax.rsqrt(jnp.mean(wide * wide, axis=-1, keepdims=True) + EPS_NORM)
    normed = (wide * recip * gain_row).astype(jnp.bfloat16)
    gate_pre = jnp.dot(normed, w_gate, preferred_element_type=jnp.float32)
    inner = jnp.dot(normed, w_in, preferred_element_type=jnp.float32)
    sigmoid = jax.nn.sigmoid(gate_pre)
    swish = gate_pre * sigmoid
    mixed = (swish * inner).astype(jnp.bfloat16)
    return (wide, recip, normed, gate_pre, inner, sigmoid, swish, mixed)


def expand(quantized, block_scale):
    rows = quantized.shape[0]
    wide = quantized.astype(jnp.float32).reshape(rows, -1, BLOCK)
    return (wide * block_scale.astype(jnp.float32)[:, :, None]).reshape(rows, -1)


def local(
    fwd_input,
    bwd_input,
    cotangent,
    send_buffer,
    recv_buffer,
    fwd_ids,
    recv_ids,
    norm_gain,
    w_gate,
    w_in,
    w_out,
):
    inputs = fwd_input[0]
    rows, width = inputs.shape
    gain_row = norm_gain[0]
    gate_w = w_gate[0]
    in_w = w_in[0]
    out_w = w_out[0]
    saved = adapter_inner(inputs, gain_row, gate_w, in_w)
    output = saved[0] + contract_cols(saved[7], out_w)
    stored = jnp.take(send_buffer[0], fwd_ids[0], axis=0).reshape(rows, width)
    difference = output - stored.astype(jnp.float32)
    blocks = difference.reshape(rows, -1, BLOCK)
    block_scale = (jnp.max(jnp.abs(blocks), axis=-1) + EPS_SCALE).astype(jnp.bfloat16)
    quantized = (
        (blocks / block_scale.astype(jnp.float32)[:, :, None])
        .astype(jnp.bfloat16)
        .reshape(rows, width)
    )
    send_rows = (stored.astype(jnp.float32) + expand(quantized, block_scale)).astype(jnp.bfloat16)
    quant_in, scale_in = passed_along((quantized, block_scale), "section", 1)
    arrived = jnp.take(recv_buffer[0], recv_ids[0], axis=0).reshape(rows, width).astype(jnp.float32)
    next_input = (arrived + expand(quant_in, scale_in)).astype(jnp.bfloat16)
    upstream_in = cotangent[0]
    backed = bwd_input[0]
    wide, recip, normed, gate_pre, inner, sigmoid, swish, mixed = adapter_inner(
        backed, gain_row, gate_w, in_w
    )
    grad_mixed = jnp.dot(upstream_in, out_w, preferred_element_type=jnp.float32)
    grad_gate = (grad_mixed * inner * sigmoid * (1.0 + gate_pre * (1.0 - sigmoid))).astype(
        jnp.bfloat16
    )
    grad_inner = (grad_mixed * swish).astype(jnp.bfloat16)
    grad_normed = contract_cols(grad_gate, gate_w) + contract_cols(grad_inner, in_w)
    scaled = grad_normed * gain_row
    grad_inputs = recip * scaled - wide * recip * recip * recip * jnp.mean(
        wide * scaled, axis=-1, keepdims=True
    )
    passed = (upstream_in.astype(jnp.float32) + grad_inputs).astype(jnp.bfloat16)
    next_cotangent = passed_along(passed, "section", -1)
    terms = jnp.concatenate(
        [
            contract_rows(normed, grad_gate),
            contract_rows(normed, grad_inner),
            contract_rows(upstream_in, mixed),
        ],
        axis=1,
    )
    gain_term = jnp.sum(grad_normed * wide * recip, axis=0)
    summed_terms, summed_gain = (
        lax.psum_scatter(terms.astype(jnp.bfloat16), "dp", scatter_dimension=0, tiled=True).astype(
            jnp.float32
        ),
        lax.psum_scatter(
            gain_term.astype(jnp.bfloat16), "dp", scatter_dimension=0, tiled=True
        ).astype(jnp.float32),
    )
    return (
        next_input[None],
        send_rows[None],
        next_cotangent[None],
        summed_terms[None],
        summed_gain[None],
    )


def solution(mesh):
    return jax.shard_map(
        local,
        mesh=mesh,
        in_specs=(
            P("section", "dp", None),
            P("section", "dp", None),
            P("section", "dp", None),
            P("section", "dp", None, None),
            P("section", "dp", None, None),
            P("section", "dp"),
            P("section", "dp"),
            P("section", None),
            P("section", None, None),
            P("section", None, None),
            P("section", None, None),
        ),
        out_specs=(
            P("section", "dp", None),
            P("section", "dp", None),
            P("section", "dp", None),
            P("section", "dp", None),
            P("section", "dp"),
        ),
        check_vma=False,
    )
```

profile of v0, /device:TPU:8, one launch (start us, length us, event | category | flops | bytes accessed | tf_op | source)
XLA Modules:
  0.0 222.9 jit_solution(10782267498918545479)
XLA Ops:
  7.2 2.2 %fusion.18 = f32[128]{0:T(128)S(1)} fusion(bf16[1,128,8192]{2,1,0:T(8,128)(2,1)} %param.14), kind=kLoop, calls=%fused_computation.31 | loop fusion | flops 3145600 | bytes 2097664 | tf_op jit(solution)/shard_map/reduce_sum | solution.py:33
  9.6 2.6 %fusion.38 = f32[128,128]{1,0:T(8,128)S(1)} fusion(bf16[1,8192,128]{2,1,0:T(8,128)(2,1)} %param.22, bf16[1,128,8192]{2,1,0:T(8,128)(2,1)S(1)} %copy-done.2, f32[128]{0:T(128)S(1)} %add_rsqrt_fusion, f32[8192]{0:T(1024)} %bitcast.151), kind=kOutput, calls=%fused_computation.55 | convolution fusion | flops 272629760 | bytes 4293120 | tf_op jit(solution)/shard_map/dot_general | solution.py:36
  12.3 0.9 fusion.44
  14.5 0.7 multiply_convert_fusion.1
  16.0 0.9 copy-done.5
  16.8 1.7 fusion.21
  18.6 2.9 %fusion.13 = bf16[128,8192]{1,0:T(8,128)(2,1)} fusion(bf16[1,128,8192]{2,1,0:T(8,128)(2,1)S(1)} %copy-done.2, f32[128,8192]{1,0:T(8,128)S(1)} %get-tuple-element.22, bf16[1,128,8192]{2,1,0:T(8,128)(2,1)S(1)} %copy-done.4, f32[128]{0:T(128)S(1)} %broadcast_multiply_fusion, f32[8192]{0:T(1024)S(1)} %bitcast.154, f32[128]{0:T(128)S(1)} %add_rsqrt_fusion), kind=kLoop, calls=%fused_computation.26 | loop fusion | flops 11534336 | bytes 10519552 | tf_op jit(solution)/shard_map/convert_element_type | solution.py:98
  21.4 3.5 %collective-permute-start.2 = (bf16[128,8192]{1,0:T(8,128)(2,1)}, bf16[128,8192]{1,0:T(8,128)(2,1)}, u32[]{:S(2)}, u32[]{:S(2)}) collective-permute-start(bf16[128,8192]{1,0:T(8,128)(2,1)} %fusion.13), channel_id=1, source_target_pairs={{16,0},{32,16},{48,32},{64,48},{80,64},{96,80},{112,96},{17,1},{33... | collective-permute-start | bytes 6291464 | tf_op jit(solution)/shard_map/ppermute | solution.py:16
  24.9 0.9 convolution_convert_fusion.1
  25.8 0.9 convolution_convert_fusion.2
  26.6 0.7 fusion.1
  27.4 7.0 %pad_maximum_fusion = bf16[8192,384]{0,1:T(8,128)(2,1)} fusion(bf16[8192,128]{0,1:T(8,128)(2,1)S(1)} %fusion.1, bf16[8192,128]{0,1:T(8,128)(2,1)S(1)} %convolution_convert_fusion.1, bf16[8192,128]{0,1:T(8,128)(2,1)S(1)} %convolution_convert_fusion.2), kind=kLoop, calls=%fused_computation.9 | loop fusion | flops 18874368 | bytes 12582912 | tf_op jit(solution)/shard_map/concatenate | solution.py:100
  35.1 2.2 fusion.15
  37.3 2.5 %fusion.46 = f32[128,128]{1,0:T(8,128)S(1)} fusion(bf16[1,8192,128]{2,1,0:T(8,128)(2,1)} %param.21, bf16[1,128,8192]{2,1,0:T(8,128)(2,1)S(1)} %copy-done.6, f32[8192]{0:T(1024)S(1)} %bitcast.157, f32[128]{0:T(128)S(1)} %add_rsqrt_fusion.1), kind=kOutput, calls=%fused_computation.63 | convolution fusion | flops 272629760 | bytes 4293120 | tf_op jit(solution)/shard_map/dot_general | solution.py:35
  39.8 2.0 gather_fusion.1
  41.8 1.9 broadcast_select_fusion
  43.6 7.4 %fusion = f32[128,8192]{1,0:T(8,128)} fusion(bf16[128,8192]{1,0:T(8,128)(2,1)S(1)} %bitcast.147, bf16[1,128,8192]{2,1,0:T(8,128)(2,1)} %param.13, bf16[1,8192,128]{2,1,0:T(8,128)(2,1)} %param.23, bf16[1,8192,128]{2,1,0:T(8,128)(2,1)} %param.22, f32[8192]{0:T(1024)S(1)} %bitcast.158, f32[128]{0:T(128)S(1)} %add_rsqrt_fusion.1, f32[128,128]{1,0:T(8,128)S(1)} %fusion.46), kind=kOutput, calls=%fused_computation.4 | convolution fusion | flops 545357824 | bytes 12681728 | tf_op jit(solution)/shard_map/dot_general | solution.py:26
  51.0 2.9 %abs_bitcast_fusion = f32[16,8,64,128]{3,1,2,0:T(8,128)S(1)} fusion(f32[128,8192]{1,0:T(8,128)} %fusion), kind=kLoop, calls=%fused_computation.44 | loop fusion | flops 1048576 | bytes 8388608
  53.9 2.8 %copy.18 = f32[16,8,64,128]{3,2,1,0:T(8,128)} copy(f32[16,8,64,128]{3,1,2,0:T(8,128)S(1)} %abs_bitcast_fusion) | data formatting | bytes 8388608
  56.7 3.7 %reduce_max.9 = f32[128,64]{1,0:T(8,128)S(1)} reduce(f32[128,64,128]{2,1,0:T(8,128)} %bitcast.150, f32[]{:T(128)} %constant.11.clone.1), dimensions={2}, to_apply=%region_1.0 | reduce | flops 1040384 | bytes 4227076 | tf_op jit(solution)/shard_map/reduce_max | solution.py:73
  60.4 2.9 %collective-permute-start.1 = (bf16[128,64]{1,0:T(8,128)(2,1)S(1)}, bf16[128,64]{1,0:T(8,128)(2,1)S(1)}, u32[]{:S(2)}, u32[]{:S(2)}) collective-permute-start(bf16[128,64]{1,0:T(8,128)(2,1)S(1)} %add_convert_fusion), channel_id=1, source_target_pairs={{0,16},{16,32},{32,48},{48,64},{64,80},{80,96},{96,112},{1,17},{17... | collective-permute-start | bytes 49160 | tf_op jit(solution)/shard_map/ppermute | solution.py:16
  63.3 1.1 div.28
  64.5 5.6 %fusion.29 = (bf16[1,128,8192]{2,1,0:T(8,128)(2,1)}, bf16[128,8192]{1,0:T(8,128)(2,1)}) fusion(f32[16,8,64,128]{3,2,1,0:T(8,128)S(1)} %bitcast.148, bf16[2,64,8192]{2,1,0:T(8,128)(2,1)S(1)} %broadcast_select_fusion, f32[128,8192]{1,0:T(8,128)S(1)} %copy-done.3), kind=kLoop, calls=%fused_computation.46 | loop fusion | flops 7340032 | bytes 14680064 | tf_op jit(solution)/shard_map/broadcast_in_dim | solution.py:119
  70.1 4.5 %collective-permute-start = (bf16[128,8192]{1,0:T(8,128)(2,1)}, bf16[128,8192]{1,0:T(8,128)(2,1)}, u32[]{:S(2)}, u32[]{:S(2)}) collective-permute-start(bf16[128,8192]{1,0:T(8,128)(2,1)} %get-tuple-element.19), channel_id=1, source_target_pairs={{0,16},{16,32},{32,48},{48,64},{64,80},{80,96},{96,112},{1,17},{17... | collective-permute-start | bytes 6291464 | tf_op jit(solution)/shard_map/ppermute | solution.py:16
  75.9 3.9 %gather_fusion = bf16[2,64,8192]{2,1,0:T(8,128)(2,1)} fusion(bf16[3,64,8192]{2,1,0:T(8,128)(2,1)} %bitcast.159, s32[1024]{0:T(1024)S(1)} %pad_clamp_fusion.1), kind=kCustom, calls=%fused_computation.clone | custom fusion | bytes 4194312 | tf_op jit(solution)/shard_map/jit(_take)/gather | solution.py:81
  79.8 121.2 %all-reduce = bf16[8192]{0:T(1024)(128)(2,1)S(1)} all-reduce(bf16[8192]{0:T(1024)(128)(2,1)S(1)} %get-tuple-element.16), channel_id=3, replica_groups=mesh['section'=8,'dp'=16] {'dp'}, use_global_device_ids=true, to_apply=%region_6.8.clone | all-reduce | flops 8192 | bytes 32768
  201.0 1.9 broadcast_select_fusion.1
  203.5 1.1 mul.155
  204.7 5.9 %fusion.28 = bf16[1,128,8192]{2,1,0:T(8,128)(2,1)} fusion(f32[16,8,64,128]{3,2,1,0:T(8,128)S(1)} %bitcast.149, bf16[128,8192]{1,0:T(8,128)(2,1)} %collective-permute-done, bf16[2,64,8192]{2,1,0:T(8,128)(2,1)S(1)} %broadcast_select_fusion.1), kind=kLoop, calls=%fused_computation.45 | loop fusion | flops 5242880 | bytes 10485760 | tf_op jit(solution)/shard_map/broadcast_in_dim | solution.py:118
  210.5 1.1 bitcast_convert_fusion
  211.6 1.2 copy.17
  212.8 3.2 %copy.30 = bf16[1,128,8192]{2,1,0:T(8,128)(2,1)} copy(bf16[1,128,8192]{2,1,0:T(8,128)(2,1)} %bitcast.18) | data formatting | bytes 4194304
  (44 shorter events, 4.2 us)
Async XLA Ops:
  7.2 32.6 %copy-start = (bf16[1,3,64,8192]{3,2,1,0:T(8,128)(2,1)S(1)}, bf16[1,3,64,8192]{3,2,1,0:T(8,128)(2,1)}, u32[]{:S(2)}) copy-start(bf16[1,3,64,8192]{3,2,1,0:T(8,128)(2,1)} %param.16) | copy-start | bytes 9437188
  7.2 203.4 %reduce-scatter.2.cloned.1.call-start = ((), (), s32[]{:S(2)}) async-start(), calls=%async_computation.1 | async-start | bytes 6684672 | tf_op jit(solution)/shard_map/reduce_scatter | solution.py:110
  7.2 2.4 %copy-start.2 = (bf16[1,128,8192]{2,1,0:T(8,128)(2,1)S(1)}, bf16[1,128,8192]{2,1,0:T(8,128)(2,1)}, u32[]{:S(2)}) copy-start(bf16[1,128,8192]{2,1,0:T(8,128)(2,1)} %param.14) | copy-start | bytes 6291460
  9.6 2.6 %copy-start.8 = (bf16[1,8192,128]{2,1,0:T(8,128)(2,1)S(1)}, bf16[1,8192,128]{2,1,0:T(8,128)(2,1)}, u32[]{:S(2)}) copy-start(bf16[1,8192,128]{2,1,0:T(8,128)(2,1)} %param.21) | copy-start | bytes 6291460
  9.6 2.7 %copy-start.9 = (f32[1,8192]{1,0:T(1,128)S(1)}, f32[1,8192]{1,0:T(1,128)}, u32[]{:S(2)}) copy-start(f32[1,8192]{1,0:T(1,128)} %param.20) | copy-start | bytes 98308
  12.3 1.6 copy-start.4
  12.3 2.2 copy-start.7
  15.2 1.6 copy-start.5
  21.4 182.1 %collective-permute-start.2 = (bf16[128,8192]{1,0:T(8,128)(2,1)}, bf16[128,8192]{1,0:T(8,128)(2,1)}, u32[]{:S(2)}, u32[]{:S(2)}) collective-permute-start(bf16[128,8192]{1,0:T(8,128)(2,1)} %fusion.13), channel_id=1, source_target_pairs={{16,0},{32,16},{48,32},{64,48},{80,64},{96,80},{112,96},{17,1},{33... | collective-permute-start | bytes 6291464 | tf_op jit(solution)/shard_map/ppermute | solution.py:16
  34.4 0.7 copy-start.10
  35.0 2.3 %copy-start.6 = (bf16[1,128,8192]{2,1,0:T(8,128)(2,1)S(1)}, bf16[1,128,8192]{2,1,0:T(8,128)(2,1)}, u32[]{:S(2)}) copy-start(bf16[1,128,8192]{2,1,0:T(8,128)(2,1)} %param.13) | copy-start | bytes 6291460
  60.3 4.1 %copy-start.3 = (f32[128,8192]{1,0:T(8,128)S(1)}, f32[128,8192]{1,0:T(8,128)}, u32[]{:S(2)}) copy-start(f32[128,8192]{1,0:T(8,128)} %fusion) | copy-start | bytes 12582916
  60.4 143.1 %collective-permute-start.1 = (bf16[128,64]{1,0:T(8,128)(2,1)S(1)}, bf16[128,64]{1,0:T(8,128)(2,1)S(1)}, u32[]{:S(2)}, u32[]{:S(2)}) collective-permute-start(bf16[128,64]{1,0:T(8,128)(2,1)S(1)} %add_convert_fusion), channel_id=1, source_target_pairs={{0,16},{16,32},{32,48},{48,64},{64,80},{80,96},{96,112},{1,17},{17... | collective-permute-start | bytes 49160 | tf_op jit(solution)/shard_map/ppermute | solution.py:16
  64.4 10.2 %copy-start.12 = (u32[128]{0:T(128)S(1)}, u32[128]{0:T(128)}, u32[]{:S(2)}) copy-start(u32[128]{0:T(128)} %constant.38) | copy-start | bytes 1540
  64.4 11.4 %copy-start.11 = (s32[1,2]{1,0:T(1,128)S(1)}, s32[1,2]{1,0:T(1,128)}, u32[]{:S(2)}) copy-start(s32[1,2]{1,0:T(1,128)} %param.19) | copy-start | bytes 28
  70.1 133.4 %collective-permute-start = (bf16[128,8192]{1,0:T(8,128)(2,1)}, bf16[128,8192]{1,0:T(8,128)(2,1)}, u32[]{:S(2)}, u32[]{:S(2)}) collective-permute-start(bf16[128,8192]{1,0:T(8,128)(2,1)} %get-tuple-element.19), channel_id=1, source_target_pairs={{0,16},{16,32},{32,48},{48,64},{64,80},{80,96},{96,112},{1,17},{17... | collective-permute-start | bytes 6291464 | tf_op jit(solution)/shard_map/ppermute | solution.py:16
  212.8 3.2 %copy-start.1 = (bf16[1,3,64,8192]{3,2,1,0:T(8,128)(2,1)S(1)}, bf16[1,3,64,8192]{3,2,1,0:T(8,128)(2,1)}, u32[]{:S(2)}) copy-start(bf16[1,3,64,8192]{3,2,1,0:T(8,128)(2,1)} %param.16) | copy-start | bytes 9437188
Sparse Core Ops, SparseCore 0:
  34.5 110.1 reduce-scatter.1
where the time goes:
time: 223 us
  blocking collectives  121 us (54%)
  other arithmetic  37.9 us (17%)
  local copies, waits for them, and re-layouts  18.9 us (8%)
  matrix products  18.9 us (8%)
  between operations  15 us (7%)
  starting transfers between devices  10.9 us (5%)
    unnamed x1, blocking collectives  121 us
    ppermute x3, starting transfers between devices, passed_along(): return lax.ppermute(block, axis, route)  10.8 us
    unnamed x30, local copies, waits for them, and re-layouts  10.8 us
    dot_general x3, matrix products, contract_cols(): lax.dot_general(left, right, (((1,), (1,)), ((), ())), preferred_element_...  9.77 us
    concatenate x1, other arithmetic, local(): jnp.concatenate([contract_rows(normed, grad_gate), contract_rows(normed,...  6.99 us
    broadcast_in_dim x1, other arithmetic, local(): next_input[None]  5.89 us
    broadcast_in_dim x1, other arithmetic, local(): send_rows[None]  5.65 us
    reduce_sum x2, other arithmetic, adapter_inner(): recip = lax.rsqrt(jnp.mean(wide * wide, axis=-1, keepdims=True) + EPS_NORM)  4.46 us
  transfers between devices with their start and end apart: 4, of which 0 were waited for; matrix products, arithmetic and copies ran while one was open for 25% of the time, Pallas kernels for 0%

commit v1 on v0

v1 whole, which is shorter than its diff:
```python
import functools

import jax
import jax.numpy as jnp
from jax import lax
from jax.experimental import pallas as pl
from jax.experimental.pallas import tpu as pltpu
from jax.sharding import PartitionSpec as P

MESH = pl.DeviceIdType.MESH
F32 = jnp.float32
BF16 = jnp.bfloat16

BLOCK = 128
EPS_NORM = 1e-05
EPS_SCALE = 1e-06

TOK = 128
HALF = 64
D = 8192
R = 128
CW = 512
NC = D // CW
PIECES = 4
PW = D // PIECES
SECTIONS = 8


def dot_nn(a, b):
    return jnp.dot(a, b, preferred_element_type=F32)


def dot_nt(a, b):
    return lax.dot_general(a, b, (((1,), (1,)), ((), ())), preferred_element_type=F32)


def at(i):
    return pl.ds(pl.multiple_of(i * CW, CW), CW)


def kernel(
    ids_f, ids_r, fin, bin_, cot, sbuf, rbuf, gain, wg, wi, wo,
    next_input, send_rows, next_cot, wgrad, ggrad,
    fin_v, bin_v, cot_v, sb_v, rb_v, gain_v, w_v, wo_v,
    acc, acc2, ss, gm, mx, gcat, grad_t, mixed_t, krow,
    fs, fr, bs, ni, sr, zero,
    part, core_in, chip, z_in, x_out, x_in, wg_v, gg_v,
    load_a, load_b, load_c, fs_s, fs_r, bs_s, bs_r, out_s, core_s, core_r, z_s, z_r, x_sem,
):
    s = lax.axis_index("section")
    d = lax.axis_index("dp")
    core = lax.rem(d, 2)
    xh = lax.rem(d // 2, 2)
    z = d // 4
    has_next = s < SECTIONS - 1
    has_prev = s > 0

    def load_piece(p):
        cols = pl.ds(p * PW, PW)
        return (
            pltpu.make_async_copy(fin.at[:, cols], fin_v.at[:, cols], load_a.at[p, 0]),
            pltpu.make_async_copy(wg.at[cols], w_v.at[cols, pl.ds(0, R)], load_a.at[p, 1]),
            pltpu.make_async_copy(wi.at[cols], w_v.at[cols, pl.ds(R, R)], load_a.at[p, 2]),
        )

    gain_load = pltpu.make_async_copy(gain, gain_v, load_b.at[0])
    wo_load = pltpu.make_async_copy(wo, wo_v, load_b.at[1])
    sb_load = pltpu.make_async_copy(sbuf, sb_v, load_b.at[2])
    bin_load = pltpu.make_async_copy(bin_, bin_v, load_b.at[3])
    cot_load = pltpu.make_async_copy(cot, cot_v, load_b.at[4])
    rb_load = pltpu.make_async_copy(rbuf, rb_v, load_b.at[5])
    gain_load.start()
    for p in range(PIECES):
        for c in load_piece(p):
            c.start()
    for c in (wo_load, sb_load, bin_load, cot_load, rb_load):
        c.start()

    bar = pltpu.get_barrier_semaphore()

    def greet(to):
        pl.semaphore_signal(bar, inc=1, device_id=to, device_id_type=MESH)

    sibling = (s, d + 1 - 2 * core)
    across = (s, d + 2 - 4 * xh)

    def z_peer(step):
        return (s, lax.rem(z + step, 4) * 4 + xh * 2 + core)

    greet(sibling)
    greet(across)
    for step in (1, 2, 3):
        greet(z_peer(step))

    greet((lax.rem(s + 1, SECTIONS), d))
    greet((lax.rem(s + SECTIONS - 1, SECTIONS), d))

    acc[...] = jnp.zeros_like(acc)
    ss[...] = jnp.zeros_like(ss)
    gain_load.wait()

    def norm_step(x_ref, c):
        cols = at(c)
        x = x_ref[:, cols].astype(F32)
        xg = (x * gain_v[:, cols]).astype(BF16)
        sq = x * x
        total = sq[:, 0:BLOCK]
        for b in range(1, CW // BLOCK):
            total += sq[:, b * BLOCK : (b + 1) * BLOCK]
        return total, dot_nn(xg, w_v[cols, :])

    for p in range(PIECES):
        for c in load_piece(p):
            c.wait()

        def f1(c, _):
            sq, prod = norm_step(fin_v, c)
            ss[...] += sq
            acc[...] += prod
            return 0

        lax.fori_loop(p * (NC // PIECES), (p + 1) * (NC // PIECES), f1, 0)

    recip = lax.rsqrt(jnp.sum(ss[...], axis=-1, keepdims=True) / D + EPS_NORM)
    gate_pre = acc[:, 0:R] * recip
    inner = acc[:, R : 2 * R] * recip
    mx[...] = (gate_pre * jax.nn.sigmoid(gate_pre) * inner).astype(BF16)

    pl.semaphore_wait(bar, 7)

    wo_load.wait()
    sb_load.wait()

    def fwd_copy(c):
        return pltpu.make_async_remote_copy(
            src_ref=fs.at[c], dst_ref=fr.at[c], send_sem=fs_s.at[c], recv_sem=fs_r.at[c],
            device_id=(s + 1, d), device_id_type=MESH,
        )

    def rows_out(c):
        return pltpu.make_async_copy(sr.at[:, at(c)], send_rows.at[:, at(c)], out_s.at[0, c])

    def f2(c, _):
        cols = at(c)
        update = dot_nt(mx[...], wo_v[cols, :])
        for h in range(2):
            rows = slice(h * HALF, (h + 1) * HALF)
            slot = ids_f[0, h]
            stored = sb_v[slot, :, cols].astype(F32)
            diff = fin_v[rows, cols].astype(F32) + update[rows] - stored
            for b in range(CW // BLOCK):
                lanes = slice(b * BLOCK, (b + 1) * BLOCK)
                part_diff = diff[:, lanes]
                top = jnp.max(jnp.abs(part_diff), axis=-1, keepdims=True)
                scale = (top + EPS_SCALE).astype(BF16).astype(F32)
                quantized = (part_diff / scale).astype(BF16)
                product = scale * quantized.astype(F32)
                fs[c, rows, lanes] = product.astype(BF16)
                lane_at = pl.ds(pl.multiple_of(c * CW + b * BLOCK, BLOCK), BLOCK)
                sr[rows, lane_at] = (stored[:, lanes] + product).astype(BF16)

        @pl.when(has_next)
        def _():
            fwd_copy(c).start()

        rows_out(c).start()
        return 0

    lax.fori_loop(0, NC, f2, 0)

    acc2[...] = jnp.zeros_like(acc2)
    ss[...] = jnp.zeros_like(ss)
    gm[...] = jnp.zeros_like(gm)
    bin_load.wait()
    cot_load.wait()

    def b1(c, _):
        sq, prod = norm_step(bin_v, c)
        ss[...] += sq
        acc2[...] += prod
        gm[...] += dot_nn(cot_v[:, at(c)], wo_v[at(c), :])
        return 0

    lax.fori_loop(0, NC, b1, 0)
    recip_b = lax.rsqrt(jnp.sum(ss[...], axis=-1, keepdims=True) / D + EPS_NORM)
    gate_b = acc2[:, 0:R] * recip_b
    inner_b = acc2[:, R : 2 * R] * recip_b
    sig = jax.nn.sigmoid(gate_b)
    swish = gate_b * sig
    grad_mixed = gm[...]
    gg = grad_mixed * inner_b * sig * (1.0 + gate_b * (1.0 - sig)) * recip_b
    gi = grad_mixed * swish * recip_b
    gcat[:, 0:R] = gg.astype(BF16)
    gcat[:, R : 2 * R] = gi.astype(BF16)
    grad_t[0:R, :] = gg.T.astype(BF16)
    grad_t[R : 2 * R, :] = gi.T.astype(BF16)
    mixed_t[...] = (swish * inner_b).T.astype(BF16)
    dots = jnp.sum(gg * gate_b + gi * inner_b, axis=-1, keepdims=True)
    krow[...] = jnp.broadcast_to(dots * recip_b * (1.0 / D), (TOK, BLOCK))

    def core_copy(i):
        return pltpu.make_async_remote_copy(
            src_ref=part.at[2 * i + 1 - core], dst_ref=core_in.at[i],
            send_sem=core_s.at[i], recv_sem=core_r.at[i],
            device_id=sibling, device_id_type=MESH,
        )

    def b3(j, _):
        cols = at(j)
        part[j, 0 : 2 * R, :] = dot_nn(grad_t[...], bin_v[:, cols]).astype(BF16)
        part[j, 2 * R : 3 * R, :] = dot_nn(mixed_t[...], cot_v[:, cols]).astype(BF16)

        @pl.when(lax.rem(j, 2) != core)
        def _():
            core_copy(j // 2).start()

        return 0

    lax.fori_loop(0, NC, b3, 0)

    def bwd_copy(c):
        return pltpu.make_async_remote_copy(
            src_ref=bs.at[c], dst_ref=next_cot.at[:, at(c)], send_sem=bs_s.at[c], recv_sem=bs_r.at[c],
            device_id=(s - 1, d), device_id_type=MESH,
        )

    def zero_out(c):
        return pltpu.make_async_copy(zero, next_cot.at[:, at(c)], out_s.at[1, c])

    zero[...] = jnp.zeros_like(zero)

    def b2(c, _):
        cols = at(c)
        grad_normed = dot_nt(gcat[...], w_v[cols, :])
        x = bin_v[:, cols].astype(F32)
        for b in range(CW // BLOCK):
            lanes = slice(b * BLOCK, (b + 1) * BLOCK)
            lane_at = pl.ds(pl.multiple_of(c * CW + b * BLOCK, BLOCK), BLOCK)
            passed = (
                cot_v[:, lane_at].astype(F32)
                + grad_normed[:, lanes] * gain_v[:, lane_at]
                - x[:, lanes] * krow[...]
            )
            bs[c, :, lanes] = passed.astype(BF16)

        @pl.when(has_prev)
        def _():
            bwd_copy(c).start()

        @pl.when(jnp.logical_not(has_next))
        def _():
            zero_out(c).start()

        return 0

    lax.fori_loop(0, NC, b2, 0)

    def z_copy(step, h, i):
        return pltpu.make_async_remote_copy(
            src_ref=chip.at[i], dst_ref=z_in.at[step - 1, h],
            send_sem=z_s.at[step - 1, h], recv_sem=z_r.at[step - 1, h],
            device_id=z_peer(step), device_id_type=MESH,
        )

    def chip_sum(k, _):
        h = jnp.where(k < 4, 1 - xh, xh)
        step = lax.rem(k + 1, 4)
        i = lax.rem(z + step, 4) * 2 + h
        core_copy(i).wait_recv()

        def rows_sum(t, _):
            rows = pl.ds(pl.multiple_of(t * 64, 64), 64)
            chip[i, rows, :] = (
                part[2 * i + core, rows, :].astype(F32) + core_in[i, rows, :].astype(F32)
            ).astype(BF16)
            return 0

        lax.fori_loop(0, 6, rows_sum, 0)

        @pl.when(step > 0)
        def _():
            z_copy(step, h, i).start()

        return 0

    lax.fori_loop(0, 8, chip_sum, 0)

    rb_load.wait()

    def input_out(c):
        return pltpu.make_async_copy(ni.at[:, at(c)], next_input.at[:, at(c)], out_s.at[2, c])

    def receive(c, _):
        @pl.when(has_prev)
        def _():
            fwd_copy(c).wait_recv()

        @pl.when(jnp.logical_not(has_prev))
        def _():
            fr[c] = jnp.zeros((TOK, CW), BF16)

        cols = at(c)
        for h in range(2):
            rows = slice(h * HALF, (h + 1) * HALF)
            arrived = rb_v[ids_r[0, h], :, cols].astype(F32)
            ni[rows, cols] = (arrived + fr[c, rows, :].astype(F32)).astype(BF16)
        input_out(c).start()
        return 0

    lax.fori_loop(0, NC, receive, 0)

    x_copy = pltpu.make_async_remote_copy(
        src_ref=x_out, dst_ref=x_in, send_sem=x_sem.at[0], recv_sem=x_sem.at[1],
        device_id=across, device_id_type=MESH,
    )

    def z_sum(h, rows):
        total = chip[2 * z + h, rows, :].astype(F32)
        for step in range(3):
            total += z_in[step, h, rows, :].astype(F32)
        return total

    for step in (1, 2, 3):
        z_copy(step, 1 - xh, 0).wait_recv()

    def other_sum(t, _):
        rows = pl.ds(pl.multiple_of(t * 64, 64), 64)
        x_out[rows, :] = z_sum(1 - xh, rows).astype(BF16)
        return 0

    lax.fori_loop(0, 6, other_sum, 0)
    x_copy.start()
    for step in (1, 2, 3):
        z_copy(step, xh, 0).wait_recv()
    x_copy.wait_recv()

    def final(t, _):
        lanes = pl.ds(pl.multiple_of(t * BLOCK, BLOCK), BLOCK)
        mine = pl.ds(pl.multiple_of(d * CW + t * BLOCK, BLOCK), BLOCK)
        gain_row = gain_v[:, mine]
        weighted = jnp.zeros((BLOCK, R), F32)
        for a in range(3):
            rows = slice(a * R, (a + 1) * R)
            total = chip[2 * z + xh, rows, lanes].astype(F32)
            for step in range(3):
                total += z_in[step, xh, rows, lanes].astype(F32)
            total += x_in[rows, lanes].astype(F32)
            if a < 2:
                w_rows = w_v[mine, a * R : (a + 1) * R].astype(F32)
                weighted += w_rows * total.T
                total = total * gain_row
            wg_v[lanes, a * R : (a + 1) * R] = total.T
        gg_v[:, lanes] = jnp.sum(weighted.T, axis=0, keepdims=True)
        return 0

    lax.fori_loop(0, CW // BLOCK, final, 0)
    wgrad_out = pltpu.make_async_copy(wg_v, wgrad, load_c.at[0])
    ggrad_out = pltpu.make_async_copy(gg_v, ggrad, load_c.at[1])
    wgrad_out.start()
    ggrad_out.start()

    x_copy.wait_send()

    def drain(c, _):
        @pl.when(has_next)
        def _():
            fwd_copy(c).wait_send()
            bwd_copy(c).wait_recv()

        @pl.when(has_prev)
        def _():
            bwd_copy(c).wait_send()

        @pl.when(jnp.logical_not(has_next))
        def _():
            zero_out(c).wait()

        rows_out(c).wait()
        input_out(c).wait()
        return 0

    lax.fori_loop(0, NC, drain, 0)

    def drain_core(i, _):
        core_copy(i).wait_send()
        return 0

    lax.fori_loop(0, 8, drain_core, 0)
    for step in (1, 2, 3):
        for h in range(2):
            z_copy(step, h, 0).wait_send()
    wgrad_out.wait()
    ggrad_out.wait()


def local(
    fwd_input, bwd_input, cotangent, send_buffer, recv_buffer,
    fwd_ids, recv_ids, norm_gain, w_gate, w_in, w_out,
):
    any_spec = pl.BlockSpec(memory_space=pl.ANY)
    smem = pl.BlockSpec(memory_space=pltpu.SMEM)
    dma = pltpu.SemaphoreType.DMA
    wide = (TOK, D)
    chunks = (NC, TOK, CW)
    block = (3 * R, CW)
    outs = pl.pallas_call(
        kernel,
        out_shape=[
            jax.ShapeDtypeStruct(wide, BF16),
            jax.ShapeDtypeStruct(wide, BF16),
            jax.ShapeDtypeStruct(wide, BF16),
            jax.ShapeDtypeStruct((CW, 3 * R), F32),
            jax.ShapeDtypeStruct((1, CW), F32),
        ],
        in_specs=[smem, smem] + [any_spec] * 9,
        out_specs=[any_spec] * 5,
        scratch_shapes=[
            pltpu.VMEM(wide, BF16),
            pltpu.VMEM(wide, BF16),
            pltpu.VMEM(wide, BF16),
            pltpu.VMEM((3, HALF, D), BF16),
            pltpu.VMEM((3, HALF, D), BF16),
            pltpu.VMEM((1, D), F32),
            pltpu.VMEM((D, 2 * R), BF16),
            pltpu.VMEM((D, R), BF16),
            pltpu.VMEM((TOK, 2 * R), F32),
            pltpu.VMEM((TOK, 2 * R), F32),
            pltpu.VMEM((TOK, BLOCK), F32),
            pltpu.VMEM((TOK, R), F32),
            pltpu.VMEM((TOK, R), BF16),
            pltpu.VMEM((TOK, 2 * R), BF16),
            pltpu.VMEM((2 * R, TOK), BF16),
            pltpu.VMEM((R, TOK), BF16),
            pltpu.VMEM((TOK, BLOCK), F32),
            pltpu.VMEM(chunks, BF16),
            pltpu.VMEM(chunks, BF16),
            pltpu.VMEM(chunks, BF16),
            pltpu.VMEM(wide, BF16),
            pltpu.VMEM(wide, BF16),
            pltpu.VMEM((TOK, CW), BF16),
            pltpu.VMEM((NC,) + block, BF16),
            pltpu.VMEM((8,) + block, BF16),
            pltpu.VMEM((8,) + block, BF16),
            pltpu.VMEM((3, 2) + block, BF16),
            pltpu.VMEM(block, BF16),
            pltpu.VMEM(block, BF16),
            pltpu.VMEM((CW, 3 * R), F32),
            pltpu.VMEM((1, CW), F32),
            dma((PIECES, 3)),
            dma((6,)),
            dma((2,)),
            dma((NC,)),
            dma((NC,)),
            dma((NC,)),
            dma((NC,)),
            dma((3, NC)),
            dma((8,)),
            dma((8,)),
            dma((3, 2)),
            dma((3, 2)),
            dma((2,)),
        ],
        compiler_params=pltpu.CompilerParams(
            collective_id=0, has_side_effects=True, vmem_limit_bytes=58 << 20
        ),
        cost_estimate=pl.CostEstimate(
            flops=2 * 11 * TOK * D * R, bytes_accessed=28 << 20, transcendentals=4 * TOK * R
        ),
    )(
        fwd_ids, recv_ids, fwd_input[0], bwd_input[0], cotangent[0], send_buffer[0],
        recv_buffer[0], norm_gain, w_gate[0], w_in[0], w_out[0],
    )
    return (outs[0][None], outs[1][None], outs[2][None], outs[3][None], outs[4])


def solution(mesh):
    return jax.shard_map(
        local,
        mesh=mesh,
        in_specs=(
            P("section", "dp", None),
            P("section", "dp", None),
            P("section", "dp", None),
            P("section", "dp", None, None),
            P("section", "dp", None, None),
            P("section", "dp"),
            P("section", "dp"),
            P("section", None),
            P("section", None, None),
            P("section", None, None),
            P("section", None, None),
        ),
        out_specs=(
            P("section", "dp", None),
            P("section", "dp", None),
            P("section", "dp", None),
            P("section", "dp", None),
            P("section", "dp"),
        ),
        check_vma=False,
    )
```

time: 223 us -> 122 us (0.55)
  blocking collectives: 121 us -> 0 us
  Pallas kernels: 0 us -> 113 us
  other arithmetic: 37.9 us -> 0 us
  matrix products: 18.9 us -> 0 us
  between operations: 15 us -> 0.66 us
  starting transfers between devices: 10.9 us -> 0 us
  local copies, waits for them, and re-layouts: 18.9 us -> 8.73 us
    unnamed x1 -> x0, blocking collectives: 121 us -> none
    pallas_call x0 -> x1, Pallas kernels: none -> 113 us  [local(): pl.pallas_call(kernel, out_shape=[jax.ShapeDtypeStruct(wide, BF16), jax.S...]
    dot_general x10 -> x0, matrix products: 18.9 us -> none  [the longest x3 9.77 us: contract_cols(): lax.dot_general(left, right, (((1,), (1,)), ((), ())), preferred_element_...]
    broadcast_in_dim x4 -> x0, other arithmetic: 13.3 us -> none  [the longest x1 5.89 us: local(): next_input[None]]
    ppermute x3 -> x0, starting transfers between devices: 10.8 us -> none  [passed_along(): return lax.ppermute(block, axis, route)]
    concatenate x1 -> x0, other arithmetic: 6.99 us -> none  [local(): jnp.concatenate([contract_rows(normed, grad_gate), contract_rows(normed,...]
    gather x2 -> x0, local copies, waits for them, and re-layouts: 5.89 us -> none  [the longest x1 3.89 us: local(): jnp.take(recv_buffer[0], recv_ids[0], axis=0).reshape(rows, width)]
    reduce_sum x2 -> x0, other arithmetic: 4.46 us -> none  [adapter_inner(): recip = lax.rsqrt(jnp.mean(wide * wide, axis=-1, keepdims=True) + EPS_NORM)]
  transfers between devices with their start and end apart: 4 -> 0, of which waited for: 0 -> 0; matrix products, arithmetic and copies ran while one was open for 25% -> 0% of each run, Pallas kernels for 0% -> 0%
where the time goes in v1:
time: 122 us
  Pallas kernels  113 us (93%)
  local copies, waits for them, and re-layouts  8.73 us (7%)
    pallas_call x1, Pallas kernels, local(): pl.pallas_call(kernel, out_shape=[jax.ShapeDtypeStruct(wide, BF16), jax.S...  113 us
    unnamed x13, local copies, waits for them, and re-layouts  8.73 us

profile of v1, /device:TPU:8, one launch (start us, length us, event | category | flops | bytes accessed | tf_op | source)
XLA Modules:
  0.0 122.0 jit_solution(7185638865581019982)
XLA Ops:
  0.6 112.6 %shard_map.146 = (bf16[128,8192]{1,0:T(8,128)(2,1)}, bf16[128,8192]{1,0:T(8,128)(2,1)}, bf16[128,8192]{1,0:T(8,128)(2,1)}, f32[512,384]{1,0:T(8,128)}, f32[1,512]{1,0:T(1,128)}) custom-call(s32[1,2]{1,0:T(1,128)} %ids_f.1, s32[1,2]{1,0:T(1,128)} %ids_r.1, bf16[128,8192]{1,0:T(8,128)(2,1)} %bitcast.14, bf16[128,8192]{1,0:T(8,128)(2,1)} %bitcast.15, ...), custom_call_target="tpu_custom_call" | custom-call | flops 2952790016 | bytes 29360128 | tf_op jit(solution)/shard_map/pallas_call | solution.py:406
  113.3 0.0 copy-start.1
  113.3 3.2 %copy.21 = bf16[1,128,8192]{2,1,0:T(8,128)(2,1)} copy(bf16[1,128,8192]{2,1,0:T(8,128)(2,1)} %bitcast.22) | data formatting | bytes 4194304
  116.5 0.0 copy-done.1
  116.5 0.0 copy-start
  116.5 1.3 %copy.22 = bf16[1,128,8192]{2,1,0:T(8,128)(2,1)} copy(bf16[1,128,8192]{2,1,0:T(8,128)(2,1)S(1)} %bitcast.21) | data formatting | bytes 4194304
  117.8 1.0 copy-done
  118.9 0.0 copy-start.2
  118.9 0.0 copy-start.3
  118.9 1.3 %copy.23 = bf16[1,128,8192]{2,1,0:T(8,128)(2,1)} copy(bf16[1,128,8192]{2,1,0:T(8,128)(2,1)S(1)} %bitcast.20) | data formatting | bytes 4194304
  120.2 0.4 copy-done.2
  120.5 0.9 copy.24
  121.4 0.0 copy-done.3
  121.4 0.6 copy.25
Async XLA Ops:
  113.3 3.3 %copy-start.1 = (bf16[128,8192]{1,0:T(8,128)(2,1)S(1)}, bf16[128,8192]{1,0:T(8,128)(2,1)}, u32[]{:S(2)}) copy-start(bf16[128,8192]{1,0:T(8,128)(2,1)} %get-tuple-element.11) | copy-start | bytes 6291460
  116.5 2.3 %copy-start = (bf16[128,8192]{1,0:T(8,128)(2,1)S(1)}, bf16[128,8192]{1,0:T(8,128)(2,1)}, u32[]{:S(2)}) copy-start(bf16[128,8192]{1,0:T(8,128)(2,1)} %get-tuple-element.12) | copy-start | bytes 6291460
  118.9 1.7 %copy-start.2 = (f32[512,384]{1,0:T(8,128)S(1)}, f32[512,384]{1,0:T(8,128)}, u32[]{:S(2)}) copy-start(f32[512,384]{1,0:T(8,128)} %get-tuple-element.13) | copy-start | bytes 2359300
  118.9 2.6 %copy-start.3 = (f32[1,512]{1,0:T(1,128)S(1)}, f32[1,512]{1,0:T(1,128)}, u32[]{:S(2)}) copy-start(f32[1,512]{1,0:T(1,128)} %get-tuple-element.24) | copy-start | bytes 6148

commit v2 on v1

v2 whole, which is shorter than its diff:
```python
import functools

import jax
import jax.numpy as jnp
from jax import lax
from jax.experimental import pallas as pl
from jax.experimental.pallas import tpu as pltpu
from jax.sharding import PartitionSpec as P

MESH = pl.DeviceIdType.MESH
F32 = jnp.float32
BF16 = jnp.bfloat16

BLOCK = 128
EPS_NORM = 1e-05
EPS_SCALE = 1e-06

TOK = 128
HALF = 64
D = 8192
R = 128
CW = 512
NC = D // CW
PIECES = 4
PW = D // PIECES
FIN, BIN, COT, WG, WI, WO = range(6)
RELAYS = 12
SECTIONS = 8
PEERS = 9
LATE = 13


def dot_nn(a, b):
    return jnp.dot(a, b, preferred_element_type=F32)


def dot_nt(a, b):
    return lax.dot_general(a, b, (((1,), (1,)), ((), ())), preferred_element_type=F32)


def at(i):
    return pl.ds(pl.multiple_of(i * CW, CW), CW)


def kernel(
    ids_f, ids_r, fin, bin_, cot, sbuf, rbuf, gain, wg, wi, wo,
    next_input, send_rows, next_cot, wgrad, ggrad,
    fin_v, bin_v, cot_v, sb_v, rb_v, gain_v, w_v, wo_v,
    acc, acc2, ss, gm, mx, gcat, grad_t, mixed_t, krow,
    fs, fr, bs, relay,
    part, core_in, chip, z_in, x_out, x_in,
    load_a, load_b, fs_s, fs_r, bs_s, bs_r, rl_s, rl_r, core_s, core_r, z_s, z_r, x_sem,
):
    s = lax.axis_index("section")
    d = lax.axis_index("dp")
    core = lax.rem(d, 2)
    xh = lax.rem(d // 2, 2)
    z = d // 4
    has_next = s < SECTIONS - 1
    has_prev = s > 0

    even = lax.rem(s, 2) == 0

    def piece(kind, p):
        cols = pl.ds(p * PW, PW)
        sem = load_a.at[kind, p]
        if kind == FIN:
            return pltpu.make_async_copy(fin.at[:, cols], fin_v.at[:, cols], sem)
        if kind == BIN:
            return pltpu.make_async_copy(bin_.at[:, cols], bin_v.at[:, cols], sem)
        if kind == COT:
            return pltpu.make_async_copy(cot.at[:, cols], cot_v.at[:, cols], sem)
        if kind == WG:
            return pltpu.make_async_copy(wg.at[cols], w_v.at[cols, pl.ds(0, R)], sem)
        if kind == WI:
            return pltpu.make_async_copy(wi.at[cols], w_v.at[cols, pl.ds(R, R)], sem)
        return pltpu.make_async_copy(wo.at[cols], wo_v.at[cols], sem)

    def start_pieces(*kinds):
        for p in range(PIECES):
            for kind in kinds:
                piece(kind, p).start()

    gain_load = pltpu.make_async_copy(gain, gain_v, load_b.at[0])
    sb_load = pltpu.make_async_copy(sbuf, sb_v, load_b.at[1])
    rb_load = pltpu.make_async_copy(rbuf, rb_v, load_b.at[2])
    gain_load.start()

    @pl.when(even)
    def _():
        start_pieces(FIN, WG, WI)
        start_pieces(WO)
        sb_load.start()

    @pl.when(jnp.logical_not(even))
    def _():
        start_pieces(BIN, WG, WI, COT, WO)

    bar = pltpu.get_barrier_semaphore()

    def greet(to):
        pl.semaphore_signal(bar, inc=1, device_id=to, device_id_type=MESH)

    sibling = (s, d + 1 - 2 * core)
    across = (s, d + 2 - 4 * xh)

    def z_peer(step):
        return (s, lax.rem(z + step, 4) * 4 + xh * 2 + core)

    greet(sibling)
    greet(across)
    for step in (1, 2, 3):
        greet(z_peer(step))

    for step in (1, 2, SECTIONS - 2, SECTIONS - 1):
        greet((lax.rem(s + step, SECTIONS), d))

    gain_load.wait()

    def norm_step(x_ref, c):
        cols = at(c)
        x = x_ref[:, cols].astype(F32)
        xg = (x * gain_v[:, cols]).astype(BF16)
        sq = x * x
        total = sq[:, 0:BLOCK]
        for b in range(1, CW // BLOCK):
            total += sq[:, b * BLOCK : (b + 1) * BLOCK]
        return total, dot_nn(xg, w_v[cols, :])

    fwd_via = jnp.where(jnp.logical_and(jnp.logical_not(even), has_next), 2 * (s + 1), 0)
    bwd_via = jnp.where(jnp.logical_and(even, has_prev), 16 - 2 * s, 0)
    fwd_relays = jnp.where(jnp.logical_not(even), 2 * (s - 1), 0)
    bwd_relays = jnp.where(jnp.logical_and(even, s <= 4), 12 - 2 * s, 0)

    def remote(src, dst, send, recv, to):
        return pltpu.make_async_remote_copy(
            src_ref=src, dst_ref=dst, send_sem=send, recv_sem=recv,
            device_id=(to, d), device_id_type=MESH,
        )

    def fwd_copy(c):
        return remote(fs.at[c], fr.at[c], fs_s.at[c], fs_r.at[c], s + 1)

    def fwd_detour(c):
        return remote(fs.at[c], relay.at[c], fs_s.at[c], rl_r.at[c], s + 2)

    def fwd_onward(c):
        return remote(relay.at[c], fr.at[c], rl_s.at[c], fs_r.at[c], s - 1)

    def bwd_copy(c):
        return remote(bs.at[c], next_cot.at[:, at(c)], bs_s.at[c], bs_r.at[c], s - 1)

    def bwd_detour(c):
        return remote(bs.at[c], relay.at[c], bs_s.at[c], rl_r.at[c], s - 2)

    def bwd_onward(c):
        return remote(relay.at[c], next_cot.at[:, at(c)], rl_s.at[c], bs_r.at[c], s + 1)

    def core_copy(i):
        return pltpu.make_async_remote_copy(
            src_ref=part.at[2 * i + 1 - core], dst_ref=core_in.at[i],
            send_sem=core_s.at[i], recv_sem=core_r.at[i],
            device_id=sibling, device_id_type=MESH,
        )

    def forward(first):
        acc[...] = jnp.zeros_like(acc)
        ss[...] = jnp.zeros_like(ss)

        def f1(c, _):
            sq, prod = norm_step(fin_v, c)
            ss[...] += sq
            acc[...] += prod
            return 0

        for p in range(PIECES):
            piece(FIN, p).wait()

            @pl.when(first)
            def _():
                piece(WG, p).wait()
                piece(WI, p).wait()

            lax.fori_loop(p * (NC // PIECES), (p + 1) * (NC // PIECES), f1, 0)

        @pl.when(first)
        def _():
            start_pieces(BIN, COT)
            rb_load.start()

        recip = lax.rsqrt(jnp.sum(ss[...], axis=-1, keepdims=True) / D + EPS_NORM)
        gate_pre = acc[:, 0:R] * recip
        inner = acc[:, R : 2 * R] * recip
        mx[...] = (gate_pre * jax.nn.sigmoid(gate_pre) * inner).astype(BF16)

        @pl.when(first)
        def _():
            for p in range(PIECES):
                piece(WO, p).wait()
            pl.semaphore_wait(bar, PEERS)

        sb_load.wait()

        def f2(c, _):
            cols = at(c)
            update = dot_nt(mx[...], wo_v[cols, :])
            for h in range(2):
                rows = slice(h * HALF, (h + 1) * HALF)
                slot = ids_f[0, h]
                stored = sb_v[slot, :, cols].astype(F32)
                diff = fin_v[rows, cols].astype(F32) + update[rows] - stored
                for b in range(CW // BLOCK):
                    lanes = slice(b * BLOCK, (b + 1) * BLOCK)
                    part_diff = diff[:, lanes]
                    top = jnp.max(jnp.abs(part_diff), axis=-1, keepdims=True)
                    scale = (top + EPS_SCALE).astype(BF16).astype(F32)
                    quantized = (part_diff / scale).astype(BF16)
                    product = scale * quantized.astype(F32)
                    fs[c, rows, lanes] = product.astype(BF16)
                    lane_at = pl.ds(pl.multiple_of(c * CW + b * BLOCK, BLOCK), BLOCK)
                    send_rows[rows, lane_at] = (stored[:, lanes] + product).astype(BF16)

            @pl.when(jnp.logical_and(has_next, c >= fwd_via))
            def _():
                fwd_copy(c).start()

            @pl.when(c < fwd_via)
            def _():
                fwd_detour(c).start()

            return 0

        lax.fori_loop(0, NC, f2, 0)

    def backward(first):
        acc2[...] = jnp.zeros_like(acc2)
        ss[...] = jnp.zeros_like(ss)
        gm[...] = jnp.zeros_like(gm)

        def b1(c, _):
            sq, prod = norm_step(bin_v, c)
            ss[...] += sq
            acc2[...] += prod
            gm[...] += dot_nn(cot_v[:, at(c)], wo_v[at(c), :])
            return 0

        for p in range(PIECES):
            piece(BIN, p).wait()
            piece(COT, p).wait()

            @pl.when(first)
            def _():
                for kind in (WG, WI, WO):
                    piece(kind, p).wait()

            lax.fori_loop(p * (NC // PIECES), (p + 1) * (NC // PIECES), b1, 0)

        @pl.when(first)
        def _():
            start_pieces(FIN)
            sb_load.start()
            rb_load.start()

        recip_b = lax.rsqrt(jnp.sum(ss[...], axis=-1, keepdims=True) / D + EPS_NORM)
        gate_b = acc2[:, 0:R] * recip_b
        inner_b = acc2[:, R : 2 * R] * recip_b
        sig = jax.nn.sigmoid(gate_b)
        swish = gate_b * sig
        grad_mixed = gm[...]
        gg = grad_mixed * inner_b * sig * (1.0 + gate_b * (1.0 - sig)) * recip_b
        gi = grad_mixed * swish * recip_b
        gcat[:, 0:R] = gg.astype(BF16)
        gcat[:, R : 2 * R] = gi.astype(BF16)
        grad_t[0:R, :] = gg.T.astype(BF16)
        grad_t[R : 2 * R, :] = gi.T.astype(BF16)
        mixed_t[...] = (swish * inner_b).T.astype(BF16)
        dots = jnp.sum(gg * gate_b + gi * inner_b, axis=-1, keepdims=True)
        krow[...] = jnp.broadcast_to(dots * recip_b * (1.0 / D), (TOK, BLOCK))

        @pl.when(first)
        def _():
            pl.semaphore_wait(bar, PEERS)

        def b2(c, _):
            cols = at(c)
            grad_normed = dot_nt(gcat[...], w_v[cols, :])
            x = bin_v[:, cols].astype(F32)
            for b in range(CW // BLOCK):
                lanes = slice(b * BLOCK, (b + 1) * BLOCK)
                lane_at = pl.ds(pl.multiple_of(c * CW + b * BLOCK, BLOCK), BLOCK)
                passed = (
                    cot_v[:, lane_at].astype(F32)
                    + grad_normed[:, lanes] * gain_v[:, lane_at]
                    - x[:, lanes] * krow[...]
                )
                bs[c, :, lanes] = passed.astype(BF16)

            @pl.when(jnp.logical_and(has_prev, c >= bwd_via))
            def _():
                bwd_copy(c).start()

            @pl.when(c < bwd_via)
            def _():
                bwd_detour(c).start()

            @pl.when(jnp.logical_not(has_next))
            def _():
                next_cot[:, cols] = jnp.zeros((TOK, CW), BF16)

            return 0

        lax.fori_loop(0, NC, b2, 0)

        def b3(j, _):
            cols = at(j)
            part[j, 0 : 2 * R, :] = dot_nn(grad_t[...], bin_v[:, cols]).astype(BF16)
            part[j, 2 * R : 3 * R, :] = dot_nn(mixed_t[...], cot_v[:, cols]).astype(BF16)

            @pl.when(lax.rem(j, 2) != core)
            def _():
                core_copy(j // 2).start()

            return 0

        lax.fori_loop(0, NC, b3, 0)

    def half(turn, _):
        @pl.when(lax.rem(s + turn, 2) == 0)
        def _():
            forward(turn == 0)

        @pl.when(lax.rem(s + turn, 2) == 1)
        def _():
            backward(turn == 0)

        return 0

    lax.fori_loop(0, 2, half, 0)

    def z_copy(step, h, i):
        return pltpu.make_async_remote_copy(
            src_ref=chip.at[i], dst_ref=z_in.at[step - 1, h],
            send_sem=z_s.at[step - 1, h], recv_sem=z_r.at[step - 1, h],
            device_id=z_peer(step), device_id_type=MESH,
        )

    def chip_sum(k, _):
        h = jnp.where(k < 4, 1 - xh, xh)
        step = lax.rem(k + 1, 4)
        i = lax.rem(z + step, 4) * 2 + h
        core_copy(i).wait_recv()

        def rows_sum(t, _):
            rows = pl.ds(pl.multiple_of(t * 64, 64), 64)
            chip[i, rows, :] = (
                part[2 * i + core, rows, :].astype(F32) + core_in[i, rows, :].astype(F32)
            ).astype(BF16)
            return 0

        lax.fori_loop(0, 6, rows_sum, 0)

        @pl.when(step > 0)
        def _():
            z_copy(step, h, i).start()

        return 0

    lax.fori_loop(0, 8, chip_sum, 0)

    def hand_on(c, _):
        @pl.when(even)
        def _():
            bwd_detour(c).wait_recv()
            bwd_onward(c).start()

        @pl.when(jnp.logical_not(even))
        def _():
            fwd_detour(c).wait_recv()
            fwd_onward(c).start()

        return 0

    lax.fori_loop(0, fwd_relays + bwd_relays, hand_on, 0)

    x_copy = pltpu.make_async_remote_copy(
        src_ref=x_out, dst_ref=x_in, send_sem=x_sem.at[0], recv_sem=x_sem.at[1],
        device_id=across, device_id_type=MESH,
    )

    def z_sum(h, rows):
        total = chip[2 * z + h, rows, :].astype(F32)
        for step in range(3):
            total += z_in[step, h, rows, :].astype(F32)
        return total

    for step in (1, 2, 3):
        z_copy(step, 1 - xh, 0).wait_recv()

    def other_sum(t, _):
        rows = pl.ds(pl.multiple_of(t * 64, 64), 64)
        x_out[rows, :] = z_sum(1 - xh, rows).astype(BF16)
        return 0

    lax.fori_loop(0, 6, other_sum, 0)
    x_copy.start()

    rb_load.wait()

    def receive(c, _):
        @pl.when(has_prev)
        def _():
            fwd_copy(c).wait_recv()

        @pl.when(jnp.logical_not(has_prev))
        def _():
            fr[c] = jnp.zeros((TOK, CW), BF16)

        cols = at(c)
        for h in range(2):
            rows = slice(h * HALF, (h + 1) * HALF)
            arrived = rb_v[ids_r[0, h], :, cols].astype(F32)
            next_input[rows, cols] = (arrived + fr[c, rows, :].astype(F32)).astype(BF16)
        return 0

    lax.fori_loop(0, LATE, receive, 0)

    for step in (1, 2, 3):
        z_copy(step, xh, 0).wait_recv()
    x_copy.wait_recv()

    def final(t, _):
        lanes = pl.ds(pl.multiple_of(t * BLOCK, BLOCK), BLOCK)
        mine = pl.ds(pl.multiple_of(d * CW + t * BLOCK, BLOCK), BLOCK)
        gain_row = gain_v[:, mine]
        weighted = jnp.zeros((BLOCK, R), F32)
        for a in range(3):
            rows = slice(a * R, (a + 1) * R)
            total = chip[2 * z + xh, rows, lanes].astype(F32)
            for step in range(3):
                total += z_in[step, xh, rows, lanes].astype(F32)
            total += x_in[rows, lanes].astype(F32)
            if a < 2:
                w_rows = w_v[mine, a * R : (a + 1) * R].astype(F32)
                weighted += w_rows * total.T
                total = total * gain_row
            wgrad[lanes, a * R : (a + 1) * R] = total.T
        ggrad[:, lanes] = jnp.sum(weighted.T, axis=0, keepdims=True)
        return 0

    lax.fori_loop(0, CW // BLOCK, final, 0)
    lax.fori_loop(LATE, NC, receive, 0)

    x_copy.wait_send()

    def drain(c, _):
        @pl.when(has_next)
        def _():
            fwd_copy(c).wait_send()
            bwd_copy(c).wait_recv()

        @pl.when(has_prev)
        def _():
            bwd_copy(c).wait_send()

        return 0

    lax.fori_loop(0, NC, drain, 0)

    def drain_relay(c, _):
        bwd_onward(c).wait_send()
        return 0

    lax.fori_loop(0, fwd_relays + bwd_relays, drain_relay, 0)

    def drain_core(i, _):
        core_copy(i).wait_send()
        return 0

    lax.fori_loop(0, 8, drain_core, 0)
    for step in (1, 2, 3):
        for h in range(2):
            z_copy(step, h, 0).wait_send()


def store(*refs):
    copies = [pltpu.make_async_copy(refs[k], refs[5 + k], refs[10].at[k]) for k in range(5)]
    for c in copies:
        c.start()
    for c in copies:
        c.wait()


def local(
    fwd_input, bwd_input, cotangent, send_buffer, recv_buffer,
    fwd_ids, recv_ids, norm_gain, w_gate, w_in, w_out,
):
    any_spec = pl.BlockSpec(memory_space=pl.ANY)
    smem = pl.BlockSpec(memory_space=pltpu.SMEM)
    dma = pltpu.SemaphoreType.DMA
    wide = (TOK, D)
    chunks = (NC, TOK, CW)
    block = (3 * R, CW)
    outs = pl.pallas_call(
        kernel,
        out_shape=[
            pltpu.VMEM(wide, BF16),
            pltpu.VMEM(wide, BF16),
            pltpu.VMEM(wide, BF16),
            pltpu.VMEM((CW, 3 * R), F32),
            pltpu.VMEM((1, CW), F32),
        ],
        in_specs=[smem, smem] + [any_spec] * 9,
        out_specs=[pl.BlockSpec(memory_space=pltpu.VMEM)] * 5,
        scratch_shapes=[
            pltpu.VMEM(wide, BF16),
            pltpu.VMEM(wide, BF16),
            pltpu.VMEM(wide, BF16),
            pltpu.VMEM((3, HALF, D), BF16),
            pltpu.VMEM((3, HALF, D), BF16),
            pltpu.VMEM((1, D), F32),
            pltpu.VMEM((D, 2 * R), BF16),
            pltpu.VMEM((D, R), BF16),
            pltpu.VMEM((TOK, 2 * R), F32),
            pltpu.VMEM((TOK, 2 * R), F32),
            pltpu.VMEM((TOK, BLOCK), F32),
            pltpu.VMEM((TOK, R), F32),
            pltpu.VMEM((TOK, R), BF16),
            pltpu.VMEM((TOK, 2 * R), BF16),
            pltpu.VMEM((2 * R, TOK), BF16),
            pltpu.VMEM((R, TOK), BF16),
            pltpu.VMEM((TOK, BLOCK), F32),
            pltpu.VMEM(chunks, BF16),
            pltpu.VMEM(chunks, BF16),
            pltpu.VMEM(chunks, BF16),
            pltpu.VMEM((RELAYS, TOK, CW), BF16),
            pltpu.VMEM((NC,) + block, BF16),
            pltpu.VMEM((8,) + block, BF16),
            pltpu.VMEM((8,) + block, BF16),
            pltpu.VMEM((3, 2) + block, BF16),
            pltpu.VMEM(block, BF16),
            pltpu.VMEM(block, BF16),
            dma((6, PIECES)),
            dma((3,)),
            dma((NC,)),
            dma((NC,)),
            dma((NC,)),
            dma((NC,)),
            dma((RELAYS,)),
            dma((RELAYS,)),
            dma((8,)),
            dma((8,)),
            dma((3, 2)),
            dma((3, 2)),
            dma((2,)),
        ],
        compiler_params=pltpu.CompilerParams(
            collective_id=0, has_side_effects=True, vmem_limit_bytes=53 << 20
        ),
        cost_estimate=pl.CostEstimate(
            flops=2 * 11 * TOK * D * R, bytes_accessed=28 << 20, transcendentals=4 * TOK * R
        ),
    )(
        fwd_ids, recv_ids, fwd_input[0], bwd_input[0], cotangent[0], send_buffer[0],
        recv_buffer[0], norm_gain, w_gate[0], w_in[0], w_out[0],
    )
    outs = pl.pallas_call(
        store,
        out_shape=[jax.ShapeDtypeStruct(o.shape, o.dtype) for o in outs],
        in_specs=[pl.BlockSpec(memory_space=pltpu.VMEM)] * 5,
        out_specs=[any_spec] * 5,
        scratch_shapes=[dma((5,))],
        compiler_params=pltpu.CompilerParams(vmem_limit_bytes=2 ** 20),
        cost_estimate=pl.CostEstimate(flops=0, bytes_accessed=7 << 20, transcendentals=0),
    )(*outs)
    return (outs[0][None], outs[1][None], outs[2][None], outs[3][None], outs[4])


def solution(mesh):
    return jax.shard_map(
        local,
        mesh=mesh,
        in_specs=(
            P("section", "dp", None),
            P("section", "dp", None),
            P("section", "dp", None),
            P("section", "dp", None, None),
            P("section", "dp", None, None),
            P("section", "dp"),
            P("section", "dp"),
            P("section", None),
            P("section", None, None),
            P("section", None, None),
            P("section", None, None),
        ),
        out_specs=(
            P("section", "dp", None),
            P("section", "dp", None),
            P("section", "dp", None),
            P("section", "dp", None),
            P("section", "dp"),
        ),
        check_vma=False,
    )
```

time: 122 us -> 105 us (0.86)
  Pallas kernels: 113 us -> 104 us
  local copies, waits for them, and re-layouts: 8.73 us -> 0 us
    pallas_call x1 -> x2, Pallas kernels: 113 us -> 104 us  [the longest x1 101 us: local(): pl.pallas_call(kernel, out_shape=[pltpu.VMEM(wide, BF16), pltpu.VMEM(wide...]
    unnamed x13 -> x0, local copies, waits for them, and re-layouts: 8.73 us -> none
where the time goes in v2:
time: 105 us
  Pallas kernels  104 us (99%)
    pallas_call x1, Pallas kernels, local(): pl.pallas_call(kernel, out_shape=[pltpu.VMEM(wide, BF16), pltpu.VMEM(wide...  101 us
    pallas_call x1, Pallas kernels, local(): pl.pallas_call(store, out_shape=[jax.ShapeDtypeStruct(o.shape, o.dtype) f...  2.94 us

profile of v2, /device:TPU:8, one launch (start us, length us, event | category | flops | bytes accessed | tf_op | source)
XLA Modules:
  0.0 104.5 jit_solution(4196117498191482299)
XLA Ops:
  0.6 101.0 %shard_map.146 = (bf16[128,8192]{1,0:T(8,128)(2,1)S(1)}, bf16[128,8192]{1,0:T(8,128)(2,1)S(1)}, bf16[128,8192]{1,0:T(8,128)(2,1)S(1)}, f32[512,384]{1,0:T(8,128)S(1)}, f32[1,512]{1,0:T(1,128)S(1)}) custom-call(s32[1,2]{1,0:T(1,128)} %ids_f.1, s32[1,2]{1,0:T(1,128)} %ids_r.1, bf16[128,8192]{1,0:T(8,128)(2,1)} %bitcast.14, bf16[128,8192]{1,0:T(8,128)(2,1)} %bitcast.15, ...), custom_call_target="tpu_custom_call" | custom-call | flops 2952790016 | bytes 29360128 | tf_op jit(solution)/shard_map/pallas_call | solution.py:503
  101.6 2.9 %shard_map.147 = (bf16[128,8192]{1,0:T(8,128)(2,1)}, bf16[128,8192]{1,0:T(8,128)(2,1)}, bf16[128,8192]{1,0:T(8,128)(2,1)}, f32[512,384]{1,0:T(8,128)}, f32[1,512]{1,0:T(1,128)}) custom-call(bf16[128,8192]{1,0:T(8,128)(2,1)S(1)} %get-tuple-element.15.refs_0_, bf16[128,8192]{1,0:T(8,128)(2,1)S(1)} %get-tuple-element.16.refs_1_, ...), custom_call_target="tpu_custom_call" | custom-call | bytes 7340032 | tf_op jit(solution)/shard_map/pallas_call | solution.py:566

commit v3 on v2

--- a/solution.py
+++ b/solution.py
@@ -23,7 +23,7 @@
 NC = D // CW
 PIECES = 4
 PW = D // PIECES
-FIN, BIN, COT, WG, WI, WO = range(6)
+FIN, BIN, COT, WG, WI, WO, SB = range(7)
 RELAYS = 12
 SECTIONS = 8
 PEERS = 9
@@ -42,14 +42,18 @@
     return pl.ds(pl.multiple_of(i * CW, CW), CW)
 
 
+def span(p):
+    return pl.ds(pl.multiple_of(p * PW, PW), PW)
+
+
 def kernel(
-    ids_f, ids_r, fin, bin_, cot, sbuf, rbuf, gain, wg, wi, wo,
+    idf, idr, fin, bin_, cot, sbuf, rbuf, gain, wg, wi, wo,
     next_input, send_rows, next_cot, wgrad, ggrad,
     fin_v, bin_v, cot_v, sb_v, rb_v, gain_v, w_v, wo_v,
     acc, acc2, ss, gm, mx, gcat, grad_t, mixed_t, krow,
     fs, fr, bs, relay,
     part, core_in, chip, z_in, x_out, x_in,
-    load_a, load_b, fs_s, fs_r, bs_s, bs_r, rl_s, rl_r, core_s, core_r, z_s, z_r, x_sem,
+    ids_f, ids_r, load_a, load_b, fs_s, fs_r, bs_s, bs_r, rl_s, rl_r, core_s, core_r, z_s, z_r, x_sem,
 ):
     s = lax.axis_index("section")
     d = lax.axis_index("dp")
@@ -62,7 +66,7 @@
     even = lax.rem(s, 2) == 0
 
     def piece(kind, p):
-        cols = pl.ds(p * PW, PW)
+        cols = span(p)
         sem = load_a.at[kind, p]
         if kind == FIN:
             return pltpu.make_async_copy(fin.at[:, cols], fin_v.at[:, cols], sem)
@@ -74,7 +78,9 @@
             return pltpu.make_async_copy(wg.at[cols], w_v.at[cols, pl.ds(0, R)], sem)
         if kind == WI:
             return pltpu.make_async_copy(wi.at[cols], w_v.at[cols, pl.ds(R, R)], sem)
-        return pltpu.make_async_copy(wo.at[cols], wo_v.at[cols], sem)
+        if kind == WO:
+            return pltpu.make_async_copy(wo.at[cols], wo_v.at[cols], sem)
+        return pltpu.make_async_copy(sbuf.at[:, :, cols], sb_v.at[:, :, cols], sem)
 
     def start_pieces(*kinds):
         for p in range(PIECES):
@@ -82,19 +88,22 @@
                 piece(kind, p).start()
 
     gain_load = pltpu.make_async_copy(gain, gain_v, load_b.at[0])
-    sb_load = pltpu.make_async_copy(sbuf, sb_v, load_b.at[1])
-    rb_load = pltpu.make_async_copy(rbuf, rb_v, load_b.at[2])
+    idf_load = pltpu.make_async_copy(idf, ids_f, load_b.at[1])
+    idr_load = pltpu.make_async_copy(idr, ids_r, load_b.at[2])
+    rb_load = pltpu.make_async_copy(rbuf, rb_v, load_b.at[3])
     gain_load.start()
 
     @pl.when(even)
     def _():
         start_pieces(FIN, WG, WI)
-        start_pieces(WO)
-        sb_load.start()
 
     @pl.when(jnp.logical_not(even))
     def _():
-        start_pieces(BIN, WG, WI, COT, WO)
+        start_pieces(BIN, WG, WI)
+        start_pieces(COT, WO)
+
+    idf_load.start()
+    idr_load.start()
 
     bar = pltpu.get_barrier_semaphore()
 
@@ -117,13 +126,13 @@
 
     gain_load.wait()
 
-    def norm_step(x_ref, c):
-        cols = at(c)
+    def norm_step(x_ref, p):
+        cols = span(p)
         x = x_ref[:, cols].astype(F32)
         xg = (x * gain_v[:, cols]).astype(BF16)
         sq = x * x
         total = sq[:, 0:BLOCK]
-        for b in range(1, CW // BLOCK):
+        for b in range(1, PW // BLOCK):
             total += sq[:, b * BLOCK : (b + 1) * BLOCK]
         return total, dot_nn(xg, w_v[cols, :])
 
@@ -139,27 +148,27 @@
         )
 
     def fwd_copy(c):
-        return remote(fs.at[c], fr.at[c], fs_s.at[c], fs_r.at[c], s + 1)
+        return remote(fs.at[c], fr.at[c], fs_s, fs_r.at[c], s + 1)
 
     def fwd_detour(c):
-        return remote(fs.at[c], relay.at[c], fs_s.at[c], rl_r.at[c], s + 2)
+        return remote(fs.at[c], relay.at[c], fs_s, rl_r.at[c], s + 2)
 
     def fwd_onward(c):
         return remote(relay.at[c], fr.at[c], rl_s.at[c], fs_r.at[c], s - 1)
 
     def bwd_copy(c):
-        return remote(bs.at[c], next_cot.at[:, at(c)], bs_s.at[c], bs_r.at[c], s - 1)
+        return remote(bs.at[c], next_cot.at[:, at(c)], bs_s, bs_r, s - 1)
 
     def bwd_detour(c):
-        return remote(bs.at[c], relay.at[c], bs_s.at[c], rl_r.at[c], s - 2)
+        return remote(bs.at[c], relay.at[c], bs_s, rl_r.at[c], s - 2)
 
     def bwd_onward(c):
-        return remote(relay.at[c], next_cot.at[:, at(c)], rl_s.at[c], bs_r.at[c], s + 1)
+        return remote(relay.at[c], next_cot.at[:, at(c)], rl_s.at[c], bs_r, s + 1)
 
     def core_copy(i):
         return pltpu.make_async_remote_copy(
             src_ref=part.at[2 * i + 1 - core], dst_ref=core_in.at[i],
-            send_sem=core_s.at[i], recv_sem=core_r.at[i],
+            send_sem=core_s, recv_sem=core_r.at[i],
             device_id=sibling, device_id_type=MESH,
         )
 
@@ -167,21 +176,24 @@
         acc[...] = jnp.zeros_like(acc)
         ss[...] = jnp.zeros_like(ss)
 
-        def f1(c, _):
-            sq, prod = norm_step(fin_v, c)
+        def f1(p, _):
+            piece(FIN, p).wait()
+
+            @pl.when(first)
+            def _():
+                piece(WG, p).wait()
+                piece(WI, p).wait()
+
+            @pl.when(jnp.logical_and(first, p == 1))
+            def _():
+                start_pieces(WO, SB)
+
+            sq, prod = norm_step(fin_v, p)
             ss[...] += sq
             acc[...] += prod
             return 0
 
-        for p in range(PIECES):
-            piece(FIN, p).wait()
-
-            @pl.when(first)
-            def _():
-                piece(WG, p).wait()
-                piece(WI, p).wait()
-
-            lax.fori_loop(p * (NC // PIECES), (p + 1) * (NC // PIECES), f1, 0)
+        lax.fori_loop(0, PIECES, f1, 0)
 
         @pl.when(first)
         def _():
@@ -195,19 +207,28 @@
 
         @pl.when(first)
         def _():
-            for p in range(PIECES):
-                piece(WO, p).wait()
             pl.semaphore_wait(bar, PEERS)
 
-        sb_load.wait()
+        idf_load.wait()
+
+        def chosen(slot, cols):
+            last = jnp.where(slot == 1, sb_v[1, :, cols], sb_v[2, :, cols])
+            return jnp.where(slot == 0, sb_v[0, :, cols], last)
 
         def f2(c, _):
+            @pl.when(lax.rem(c, NC // PIECES) == 0)
+            def _():
+                piece(SB, c // (NC // PIECES)).wait()
+
+                @pl.when(first)
+                def _():
+                    piece(WO, c // (NC // PIECES)).wait()
+
             cols = at(c)
             update = dot_nt(mx[...], wo_v[cols, :])
             for h in range(2):
                 rows = slice(h * HALF, (h + 1) * HALF)
-                slot = ids_f[0, h]
-                stored = sb_v[slot, :, cols].astype(F32)
+                stored = chosen(ids_f[0, h], cols).astype(F32)
                 diff = fin_v[rows, cols].astype(F32) + update[rows] - stored
                 for b in range(CW // BLOCK):
                     lanes = slice(b * BLOCK, (b + 1) * BLOCK)
@@ -237,28 +258,36 @@
         ss[...] = jnp.zeros_like(ss)
         gm[...] = jnp.zeros_like(gm)
 
-        def b1(c, _):
-            sq, prod = norm_step(bin_v, c)
+        def b1(p, _):
+            piece(BIN, p).wait()
+
+            @pl.when(first)
+            def _():
+                piece(WG, p).wait()
+                piece(WI, p).wait()
+
+            sq, prod = norm_step(bin_v, p)
             ss[...] += sq
             acc2[...] += prod
-            gm[...] += dot_nn(cot_v[:, at(c)], wo_v[at(c), :])
             return 0
 
-        for p in range(PIECES):
-            piece(BIN, p).wait()
+        lax.fori_loop(0, PIECES, b1, 0)
+
+        def b1_mixed(p, _):
             piece(COT, p).wait()
 
             @pl.when(first)
             def _():
-                for kind in (WG, WI, WO):
-                    piece(kind, p).wait()
-
-            lax.fori_loop(p * (NC // PIECES), (p + 1) * (NC // PIECES), b1, 0)
+                piece(WO, p).wait()
+
+            gm[...] += dot_nn(cot_v[:, span(p)], wo_v[span(p), :])
+            return 0
+
+        lax.fori_loop(0, PIECES, b1_mixed, 0)
 
         @pl.when(first)
         def _():
-            start_pieces(FIN)
-            sb_load.start()
+            start_pieces(FIN, SB)
             rb_load.start()
 
         recip_b = lax.rsqrt(jnp.sum(ss[...], axis=-1, keepdims=True) / D + EPS_NORM)
@@ -340,7 +369,7 @@
     def z_copy(step, h, i):
         return pltpu.make_async_remote_copy(
             src_ref=chip.at[i], dst_ref=z_in.at[step - 1, h],
-            send_sem=z_s.at[step - 1, h], recv_sem=z_r.at[step - 1, h],
+            send_sem=z_s, recv_sem=z_r.at[step - 1, h],
             device_id=z_peer(step), device_id_type=MESH,
         )
 
@@ -404,9 +433,13 @@
     lax.fori_loop(0, 6, other_sum, 0)
     x_copy.start()
 
+    fwd_late = jnp.where(even, 2 * s, 0)
     rb_load.wait()
-
-    def receive(c, _):
+    idr_load.wait()
+
+    def receive(k, _):
+        c = lax.rem(k + fwd_late, NC)
+
         @pl.when(has_prev)
         def _():
             fwd_copy(c).wait_recv()
@@ -452,34 +485,29 @@
 
     x_copy.wait_send()
 
-    def drain(c, _):
-        @pl.when(has_next)
-        def _():
-            fwd_copy(c).wait_send()
-            bwd_copy(c).wait_recv()
-
-        @pl.when(has_prev)
-        def _():
-            bwd_copy(c).wait_send()
-
-        return 0
-
-    lax.fori_loop(0, NC, drain, 0)
+    def ended(src, send):
+        pltpu.make_async_copy(src, src, send).wait()
+
+    ended(part.at[pl.ds(0, 8)], core_s)
+    ended(part.at[pl.ds(0, 6)], z_s)
 
     def drain_relay(c, _):
         bwd_onward(c).wait_send()
         return 0
 
+    @pl.when(has_next)
+    def _():
+        ended(fs, fs_s)
+
     lax.fori_loop(0, fwd_relays + bwd_relays, drain_relay, 0)
 
-    def drain_core(i, _):
-        core_copy(i).wait_send()
-        return 0
-
-    lax.fori_loop(0, 8, drain_core, 0)
-    for step in (1, 2, 3):
-        for h in range(2):
-            z_copy(step, h, 0).wait_send()
+    @pl.when(has_prev)
+    def _():
+        ended(bs, bs_s)
+
+    @pl.when(has_next)
+    def _():
+        ended(next_cot, bs_r)
 
 
 def store(*refs):
@@ -495,7 +523,6 @@
     fwd_ids, recv_ids, norm_gain, w_gate, w_in, w_out,
 ):
     any_spec = pl.BlockSpec(memory_space=pl.ANY)
-    smem = pl.BlockSpec(memory_space=pltpu.SMEM)
     dma = pltpu.SemaphoreType.DMA
     wide = (TOK, D)
     chunks = (NC, TOK, CW)
@@ -509,7 +536,7 @@
             pltpu.VMEM((CW, 3 * R), F32),
             pltpu.VMEM((1, CW), F32),
         ],
-        in_specs=[smem, smem] + [any_spec] * 9,
+        in_specs=[any_spec] * 11,
         out_specs=[pl.BlockSpec(memory_space=pltpu.VMEM)] * 5,
         scratch_shapes=[
             pltpu.VMEM(wide, BF16),
@@ -539,17 +566,19 @@
             pltpu.VMEM((3, 2) + block, BF16),
             pltpu.VMEM(block, BF16),
             pltpu.VMEM(block, BF16),
-            dma((6, PIECES)),
-            dma((3,)),
+            pltpu.SMEM((1, 2), jnp.int32),
+            pltpu.SMEM((1, 2), jnp.int32),
+            dma((7, PIECES)),
+            dma((4,)),
+            dma,
             dma((NC,)),
-            dma((NC,)),
-            dma((NC,)),
-            dma((NC,)),
+            dma,
+            dma,
             dma((RELAYS,)),
             dma((RELAYS,)),
+            dma,
             dma((8,)),
-            dma((8,)),
-            dma((3, 2)),
+            dma,
             dma((3, 2)),
             dma((2,)),
         ],

time: 105 us -> 102 us (0.971)
  Pallas kernels: 104 us -> 100 us
    pallas_call x1, Pallas kernels: 101 us -> 97.4 us  [local(): pl.pallas_call(kernel, out_shape=[pltpu.VMEM(wide, BF16), pltpu.VMEM(wide...]
where the time goes in v3:
time: 102 us; the launch traced here: 101 us
  Pallas kernels  100 us (98%)
    pallas_call x1, Pallas kernels, local(): pl.pallas_call(kernel, out_shape=[pltpu.VMEM(wide, BF16), pltpu.VMEM(wide...  97.4 us
    pallas_call x1, Pallas kernels, local(): pl.pallas_call(store, out_shape=[jax.ShapeDtypeStruct(o.shape, o.dtype) f...  2.94 us

profile of v3, /device:TPU:8, one launch (start us, length us, event | category | flops | bytes accessed | tf_op | source)
XLA Modules:
  0.0 101.0 jit_solution(9481345039163600656)
XLA Ops:
  0.6 97.4 %shard_map.146 = (bf16[128,8192]{1,0:T(8,128)(2,1)S(1)}, bf16[128,8192]{1,0:T(8,128)(2,1)S(1)}, bf16[128,8192]{1,0:T(8,128)(2,1)S(1)}, f32[512,384]{1,0:T(8,128)S(1)}, f32[1,512]{1,0:T(1,128)S(1)}) custom-call(s32[1,2]{1,0:T(1,128)} %idf.1, s32[1,2]{1,0:T(1,128)} %idr.1, bf16[128,8192]{1,0:T(8,128)(2,1)} %bitcast.14, bf16[128,8192]{1,0:T(8,128)(2,1)} %bitcast.15, ...), custom_call_target="tpu_custom_call" | custom-call | flops 2952790016 | bytes 29360128 | tf_op jit(solution)/shard_map/pallas_call | solution.py:530
  98.0 2.9 %shard_map.147 = (bf16[128,8192]{1,0:T(8,128)(2,1)}, bf16[128,8192]{1,0:T(8,128)(2,1)}, bf16[128,8192]{1,0:T(8,128)(2,1)}, f32[512,384]{1,0:T(8,128)}, f32[1,512]{1,0:T(1,128)}) custom-call(bf16[128,8192]{1,0:T(8,128)(2,1)S(1)} %get-tuple-element.15.refs_0_, bf16[128,8192]{1,0:T(8,128)(2,1)S(1)} %get-tuple-element.16.refs_1_, ...), custom_call_target="tpu_custom_call" | custom-call | bytes 7340032 | tf_op jit(solution)/shard_map/pallas_call | solution.py:595

commit v4 on v3

--- a/solution.py
+++ b/solution.py
@@ -27,7 +27,8 @@
 RELAYS = 12
 SECTIONS = 8
 PEERS = 9
-LATE = 13
+HELD = 12
+LATE = 9
 
 
 def dot_nn(a, b):
@@ -99,8 +100,7 @@
 
     @pl.when(jnp.logical_not(even))
     def _():
-        start_pieces(BIN, WG, WI)
-        start_pieces(COT, WO)
+        start_pieces(BIN, WG, WI, COT, WO)
 
     idf_load.start()
     idr_load.start()
@@ -241,7 +241,7 @@
                     lane_at = pl.ds(pl.multiple_of(c * CW + b * BLOCK, BLOCK), BLOCK)
                     send_rows[rows, lane_at] = (stored[:, lanes] + product).astype(BF16)
 
-            @pl.when(jnp.logical_and(has_next, c >= fwd_via))
+            @pl.when(jnp.logical_and(has_next, jnp.logical_and(c >= fwd_via, jnp.logical_or(even, c < HELD))))
             def _():
                 fwd_copy(c).start()
 
@@ -260,30 +260,21 @@
 
         def b1(p, _):
             piece(BIN, p).wait()
+            piece(COT, p).wait()
 
             @pl.when(first)
             def _():
-                piece(WG, p).wait()
-                piece(WI, p).wait()
+                for kind in (WG, WI, WO):
+                    piece(kind, p).wait()
 
             sq, prod = norm_step(bin_v, p)
+            mixed_prod = dot_nn(cot_v[:, span(p)], wo_v[span(p), :])
             ss[...] += sq
             acc2[...] += prod
+            gm[...] += mixed_prod
             return 0
 
         lax.fori_loop(0, PIECES, b1, 0)
-
-        def b1_mixed(p, _):
-            piece(COT, p).wait()
-
-            @pl.when(first)
-            def _():
-                piece(WO, p).wait()
-
-            gm[...] += dot_nn(cot_v[:, span(p)], wo_v[span(p), :])
-            return 0
-
-        lax.fori_loop(0, PIECES, b1_mixed, 0)
 
         @pl.when(first)
         def _():
@@ -300,9 +291,9 @@
         gi = grad_mixed * swish * recip_b
         gcat[:, 0:R] = gg.astype(BF16)
         gcat[:, R : 2 * R] = gi.astype(BF16)
-        grad_t[0:R, :] = gg.T.astype(BF16)
-        grad_t[R : 2 * R, :] = gi.T.astype(BF16)
-        mixed_t[...] = (swish * inner_b).T.astype(BF16)
+        acc2[:, 0:R] = gg
+        acc2[:, R : 2 * R] = gi
+        gm[...] = swish * inner_b
         dots = jnp.sum(gg * gate_b + gi * inner_b, axis=-1, keepdims=True)
         krow[...] = jnp.broadcast_to(dots * recip_b * (1.0 / D), (TOK, BLOCK))
 
@@ -324,7 +315,7 @@
                 )
                 bs[c, :, lanes] = passed.astype(BF16)
 
-            @pl.when(jnp.logical_and(has_prev, c >= bwd_via))
+            @pl.when(jnp.logical_and(has_prev, jnp.logical_and(c >= bwd_via, jnp.logical_or(jnp.logical_not(even), c < HELD))))
             def _():
                 bwd_copy(c).start()
 
@@ -339,6 +330,10 @@
             return 0
 
         lax.fori_loop(0, NC, b2, 0)
+
+        grad_t[0:R, :] = acc2[:, 0:R].T.astype(BF16)
+        grad_t[R : 2 * R, :] = acc2[:, R : 2 * R].T.astype(BF16)
+        mixed_t[...] = gm[...].T.astype(BF16)
 
         def b3(j, _):
             cols = at(j)
@@ -409,7 +404,8 @@
 
         return 0
 
-    lax.fori_loop(0, fwd_relays + bwd_relays, hand_on, 0)
+    relays = fwd_relays + bwd_relays
+    lax.fori_loop(0, relays - 4, hand_on, 0)
 
     x_copy = pltpu.make_async_remote_copy(
         src_ref=x_out, dst_ref=x_in, send_sem=x_sem.at[0], recv_sem=x_sem.at[1],
@@ -432,6 +428,20 @@
 
     lax.fori_loop(0, 6, other_sum, 0)
     x_copy.start()
+
+    def send_held(c, _):
+        @pl.when(jnp.logical_and(even, has_prev))
+        def _():
+            bwd_copy(c).start()
+
+        @pl.when(jnp.logical_and(jnp.logical_not(even), has_next))
+        def _():
+            fwd_copy(c).start()
+
+        return 0
+
+    lax.fori_loop(HELD, NC, send_held, 0)
+    lax.fori_loop(jnp.maximum(relays - 4, 0), relays, hand_on, 0)
 
     fwd_late = jnp.where(even, 2 * s, 0)
     rb_load.wait()
@@ -499,7 +509,7 @@
     def _():
         ended(fs, fs_s)
 
-    lax.fori_loop(0, fwd_relays + bwd_relays, drain_relay, 0)
+    lax.fori_loop(0, relays, drain_relay, 0)
 
     @pl.when(has_prev)
     def _():

time: 102 us -> 99.8 us (0.978)
    pallas_call x1, Pallas kernels: 97.4 us -> 96.1 us  [local(): pl.pallas_call(kernel, out_shape=[pltpu.VMEM(wide, BF16), pltpu.VMEM(wide...]
where the time goes in v4:
time: 99.8 us; the launch traced here: 99.7 us
  Pallas kernels  99.1 us (99%)
    pallas_call x1, Pallas kernels, local(): pl.pallas_call(kernel, out_shape=[pltpu.VMEM(wide, BF16), pltpu.VMEM(wide...  96.1 us
    pallas_call x1, Pallas kernels, local(): pl.pallas_call(store, out_shape=[jax.ShapeDtypeStruct(o.shape, o.dtype) f...  2.94 us

profile of v4, /device:TPU:8, one launch (start us, length us, event | category | flops | bytes accessed | tf_op | source)
XLA Modules:
  0.0 99.7 jit_solution(7568324832805413736)
XLA Ops:
  0.6 96.1 %shard_map.146 = (bf16[128,8192]{1,0:T(8,128)(2,1)S(1)}, bf16[128,8192]{1,0:T(8,128)(2,1)S(1)}, bf16[128,8192]{1,0:T(8,128)(2,1)S(1)}, f32[512,384]{1,0:T(8,128)S(1)}, f32[1,512]{1,0:T(1,128)S(1)}) custom-call(s32[1,2]{1,0:T(1,128)} %idf.1, s32[1,2]{1,0:T(1,128)} %idr.1, bf16[128,8192]{1,0:T(8,128)(2,1)} %bitcast.14, bf16[128,8192]{1,0:T(8,128)(2,1)} %bitcast.15, ...), custom_call_target="tpu_custom_call" | custom-call | flops 2952790016 | bytes 29360128 | tf_op jit(solution)/shard_map/pallas_call | solution.py:540
  96.8 2.9 %shard_map.147 = (bf16[128,8192]{1,0:T(8,128)(2,1)}, bf16[128,8192]{1,0:T(8,128)(2,1)}, bf16[128,8192]{1,0:T(8,128)(2,1)}, f32[512,384]{1,0:T(8,128)}, f32[1,512]{1,0:T(1,128)}) custom-call(bf16[128,8192]{1,0:T(8,128)(2,1)S(1)} %get-tuple-element.15.refs_0_, bf16[128,8192]{1,0:T(8,128)(2,1)S(1)} %get-tuple-element.16.refs_1_, ...), custom_call_target="tpu_custom_call" | custom-call | bytes 7340032 | tf_op jit(solution)/shard_map/pallas_call | solution.py:605

commit v5 on v4

--- a/solution.py
+++ b/solution.py
@@ -21,13 +21,13 @@
 R = 128
 CW = 512
 NC = D // CW
-PIECES = 4
+PIECES = 8
 PW = D // PIECES
 FIN, BIN, COT, WG, WI, WO, SB = range(7)
 RELAYS = 12
 SECTIONS = 8
 PEERS = 9
-HELD = 12
+HELD = 13
 LATE = 9
 
 

time: 99.8 us -> 99.1 us (level)
  no operation moved by 1% of the time
where the time goes in v5:
time: 99.1 us; the launch traced here: 98.9 us
  Pallas kernels  98.3 us (99%)
    pallas_call x1, Pallas kernels, local(): pl.pallas_call(kernel, out_shape=[pltpu.VMEM(wide, BF16), pltpu.VMEM(wide...  95.3 us
    pallas_call x1, Pallas kernels, local(): pl.pallas_call(store, out_shape=[jax.ShapeDtypeStruct(o.shape, o.dtype) f...  2.94 us

profile of v5, /device:TPU:8, one launch (start us, length us, event | category | flops | bytes accessed | tf_op | source)
XLA Modules:
  0.0 98.9 jit_solution(8440142529277570100)
XLA Ops:
  0.6 95.3 %shard_map.146 = (bf16[128,8192]{1,0:T(8,128)(2,1)S(1)}, bf16[128,8192]{1,0:T(8,128)(2,1)S(1)}, bf16[128,8192]{1,0:T(8,128)(2,1)S(1)}, f32[512,384]{1,0:T(8,128)S(1)}, f32[1,512]{1,0:T(1,128)S(1)}) custom-call(s32[1,2]{1,0:T(1,128)} %idf.1, s32[1,2]{1,0:T(1,128)} %idr.1, bf16[128,8192]{1,0:T(8,128)(2,1)} %bitcast.14, bf16[128,8192]{1,0:T(8,128)(2,1)} %bitcast.15, ...), custom_call_target="tpu_custom_call" | custom-call | flops 2952790016 | bytes 29360128 | tf_op jit(solution)/shard_map/pallas_call | solution.py:540
  96.0 2.9 %shard_map.147 = (bf16[128,8192]{1,0:T(8,128)(2,1)}, bf16[128,8192]{1,0:T(8,128)(2,1)}, bf16[128,8192]{1,0:T(8,128)(2,1)}, f32[512,384]{1,0:T(8,128)}, f32[1,512]{1,0:T(1,128)}) custom-call(bf16[128,8192]{1,0:T(8,128)(2,1)S(1)} %get-tuple-element.15.refs_0_, bf16[128,8192]{1,0:T(8,128)(2,1)S(1)} %get-tuple-element.16.refs_1_, ...), custom_call_target="tpu_custom_call" | custom-call | bytes 7340032 | tf_op jit(solution)/shard_map/pallas_call | solution.py:605
